TPU v7x, 32 devices: a whole 2x2x4 slice. The times are simulated.
32 devices in a mesh: groups: 2 (over y), dp: 4 (over z), mp: 2 (over x), sub: 2 (over core).
Axes of the slice: x: 2, y: 2, z: 4, core: 2. Of those that a mesh axis runs over, the one named last changes fastest.
Arguments:
- upstream: bfloat16 [4096, 4096], P(('groups', 'dp')), parts along dimension 0, may hold values from -6 to 6
- attn: bfloat16 [4096, 4096], P(('groups', 'dp'), ('mp', 'sub')), parts along dimension 0, may hold values from -6 to 6
- gate: bfloat16 [8, 4096], P(('groups', 'dp')), parts along dimension 0, may hold values from -4 to 4
- visible: int32 [8], P(('groups', 'dp')), parts along dimension 0, may hold values from 1 to 3, as said below
- proj_weight: bfloat16 [4096, 4096], P(('mp', 'sub'), 'dp'), may hold values from -0.09375 to 0.09375
Outputs:
- grad_attn: bfloat16 [4096, 4096], P(('groups', 'dp'), ('mp', 'sub')), parts along dimension 0
- grad_weight: bfloat16 [4096, 8192], P(('mp', 'sub'), ('groups', 'dp')), parts along dimension 1
There are 2 independent parts, one for each index of `groups`. A program takes and returns all parts, laid end to end along the dimension named above; an argument that names none is the same for every part. Nothing has to cross between parts.
Inputs may be any that keep to these rules, and one draw needn't show every extreme that they name: Images i and i + 4 / 2 (for i below 2) have at most 4 visible blocks together; some image has exactly 3.
All inputs are finite; a program needn't handle non-finite values.
Results may differ from a plain program's by a relative error of at most 0.005.
Values may be sent and summed in bfloat16 or wider, within the bound.
A program may use at most 128 MiB of HBM per device.

v0:
```python
import jax
import jax.numpy as jnp
from jax import lax
from jax.sharding import PartitionSpec as P

BLOCK = 128


def per_device(upstream, attn, gate, visible, proj_weight):
    slots = upstream.shape[0]
    dp_count = lax.axis_size("dp")
    slot = lax.broadcasted_iota(jnp.int32, (slots, 1), 0)
    live = slot < BLOCK * visible[0]
    grad_proj = jnp.where(
        live, gate.astype(jnp.float32) * upstream.astype(jnp.float32), 0.0
    ).astype(jnp.bfloat16)
    columns = grad_proj
    grad_attn = lax.dot_general(
        columns,
        lax.all_gather(proj_weight, "dp", axis=1, tiled=True),
        (((1,), (1,)), ((), ())),
        preferred_element_type=jnp.float32,
    ).astype(jnp.bfloat16)
    scale = 1.0 / jnp.sqrt(jnp.float32(slots * dp_count))
    columns = grad_proj
    summed = lax.psum_scatter(
        lax.dot_general(
            columns, attn, (((0,), (0,)), ((), ())), preferred_element_type=jnp.float32
        ),
        "dp",
        scatter_dimension=0,
        tiled=True,
    )
    grad_weight = (summed.T * scale).astype(jnp.bfloat16)
    return (grad_attn, grad_weight)


def solution(mesh):
    return jax.shard_map(
        per_device,
        mesh=mesh,
        in_specs=(
            P(("groups", "dp"), None),
            P(("groups", "dp"), ("mp", "sub")),
            P(("groups", "dp"), None),
            P(("groups", "dp")),
            P(("mp", "sub"), "dp"),
        ),
        out_specs=(P(("groups", "dp"), ("mp", "sub")), P(("mp", "sub"), ("groups", "dp"))),
        check_vma=False,
    )
```

profile of v0, /device:TPU:0, one launch (start us, length us, event | category | flops | bytes accessed | tf_op | source)
XLA Modules:
  0.0 455.0 jit_solution(372967759582691257)
XLA Ops:
  7.2 0.0 copy-start
  7.2 0.0 all-gather.2.cloned.1.call-start
  7.2 0.7 all-gather.2.cloned.1.call-update
  7.9 0.0 reduce-scatter.2.cloned.1.call-start
  8.0 0.7 mul.26
  9.4 0.0 copy-done
  9.4 10.8 %fusion.1 = f32[4096,1024]{1,0:T(8,128)} fusion(bf16[512,1024]{1,0:T(8,128)(2,1)S(1)} %copy-done, bf16[512,4096]{1,0:T(8,128)(2,1)} %param.5, f32[4096]{0:T(1024)S(1)} %bitcast.6, pred[512]{0:T(512)(128)(4,1)S(1)} %iota_compare_fusion), kind=kOutput, calls=%fused_computation.4 | convolution fusion | flops 4303355904 | bytes 22036992 | tf_op jit(solution)/shard_map/dot_general | solution.py:27
  20.2 0.0 reduce-scatter.2.cloned.1.call-update
  20.2 141.8 %all-gather.2.cloned.1.call-done = bf16[1024,4096]{1,0:T(8,128)(2,1)} async-done(((bf16[1024,1024]{1,0:T(8,128)(2,1)}), bf16[1024,4096]{1,0:T(8,128)(2,1)}) %all-gather.2.cloned.1.call-update) | async-done | bytes 8388624 | tf_op jit(solution)/shard_map/all_gather | solution.py:20
  162.0 10.2 %convolution_convert_fusion = bf16[512,1024]{1,0:T(8,128)(2,1)} fusion(bf16[1024,4096]{1,0:T(8,128)(2,1)} %all-gather.2.cloned.1.call-done, bf16[512,4096]{1,0:T(8,128)(2,1)} %param.5, f32[4096]{0:T(1024)S(1)} %bitcast.7, pred[512]{0:T(512)(128)(4,1)S(1)} %iota_compare_fusion), kind=kOutput, calls=%fused_computation.3 | convolution fusion | flops 4303880192 | bytes 13648384 | tf_op jit(solution)/shard_map/dot_general | solution.py:18
  172.1 270.7 %reduce-scatter.2.cloned.1.call-done = f32[1024,1024]{1,0:T(8,128)} async-done(((f32[4096,1024]{1,0:T(8,128)}), f32[1024,1024]{1,0:T(8,128)}) %reduce-scatter.2.cloned.1.call-update) | async-done | bytes 4194320 | tf_op jit(solution)/shard_map/reduce_scatter | solution.py:26
  442.8 2.8 fusion
  445.6 2.6 copy.7
  (1 shorter events, 0.0 us)
Async XLA Ops:
  7.2 2.2 copy-start
  7.2 154.8 %all-gather.2.cloned.1.call-start = ((), (), s32[]{:S(2)}) async-start(), calls=%async_computation.1 | async-start | bytes 10485760 | tf_op jit(solution)/shard_map/all_gather | solution.py:20
  7.9 434.9 %reduce-scatter.2.cloned.1.call-start = ((), (), s32[]{:S(2)}) async-start(), calls=%async_computation.2 | async-start | bytes 20971520 | tf_op jit(solution)/shard_map/reduce_scatter | solution.py:26
Sparse Core Ops, SparseCore 0:
  9.6 152.3 all-gather.1
  164.3 278.4 reduce-scatter.1
where the time goes:
time: 455 us
  waiting for transfers between devices  413 us (91%)
  matrix products  21 us (5%)
  between operations  14.7 us (3%)
    reduce_scatter x1, waiting for transfers between devices, per_device(): lax.psum_scatter(lax.dot_general(columns, attn, (((0,), (0,)), ((), ())),...  271 us
    all_gather x1, waiting for transfers between devices, per_device(): lax.all_gather(proj_weight, 'dp', axis=1, tiled=True)  142 us
    dot_general x1, matrix products, per_device(): lax.dot_general(columns, attn, (((0,), (0,)), ((), ())), preferred_elemen...  10.8 us
    dot_general x1, matrix products, per_device(): lax.dot_general(columns, lax.all_gather(proj_weight, 'dp', axis=1, tiled=...  10.2 us
  transfers between devices with their start and end apart: 2, of which 2 were waited for; matrix products, arithmetic and copies ran while one was open for 5% of the time, Pallas kernels for 0%

commit v1 on v0

v1 whole, which is shorter than its diff:
```python
import functools

import jax
import jax.numpy as jnp
import numpy as np
from jax import lax
from jax.experimental import pallas as pl
from jax.experimental.pallas import tpu as pltpu
from jax.sharding import PartitionSpec as P

BLOCK = 128
BLOCKS = 4
LIVE = 3
PIECES = 4
MESH = pl.DeviceIdType.MESH
F32 = jnp.float32
BF16 = jnp.bfloat16


def kernel(
    n, scale,
    up_ref, attn_ref, gate_ref, visible_ref, w_ref,
    ga_ref, gw_ref,
    uq, uc, attn, w, gq, gp, part, total, up_in, up_out, dn_in, dn_out,
    load_sem, gp_send, gp_recv, sh_send, sh_recv, up_send, up_recv, dn_send, dn_recv,
):
    half = n // 2
    heads, cols = w_ref.shape
    tile = min(256, heads)
    d = lax.axis_index("dp")
    mp = lax.axis_index("mp")
    sub = lax.axis_index("sub")
    mbit = mp % 2
    q = 2 * mbit + sub
    low = (d < half).astype(jnp.int32)
    visible = visible_ref[0]

    def base(image):
        return (image >= half).astype(jnp.int32)

    def block_of(slot):
        return low * slot + (1 - low) * (BLOCKS - 1 - slot)

    def live(slot):
        return (block_of(slot) < visible).astype(F32)

    def peer(r):
        other_m = mp + (r // 2) * (1 - 2 * mbit)
        other_s = sub + (r % 2) * (1 - 2 * sub)
        return {"mp": other_m, "sub": other_s}

    def piece_of(r):
        return 2 * (mbit + (r // 2) * (1 - 2 * mbit)) + sub + (r % 2) * (1 - 2 * sub)

    my_base = base(d)
    loads = []
    for t in range(LIVE):
        b = block_of(my_base + t)
        loads.append(pltpu.make_async_copy(up_ref.at[b, q], uq.at[t], load_sem.at[t]))
    own_cols = pl.ds(pl.multiple_of(d * cols, cols), cols)
    for t in range(LIVE):
        b = block_of(my_base + t)
        loads.append(pltpu.make_async_copy(up_ref.at[b, :, :, own_cols], uc.at[t], load_sem.at[LIVE + t]))
    loads.append(pltpu.make_async_copy(w_ref, w, load_sem.at[2 * LIVE]))
    for s in range(BLOCKS):
        loads.append(pltpu.make_async_copy(attn_ref.at[block_of(s)], attn.at[s], load_sem.at[2 * LIVE + 1 + s]))
    for load in loads:
        load.start()

    barrier = pltpu.get_barrier_semaphore()
    for k in range(1, n):
        pl.semaphore_signal(barrier, inc=1, device_id={"dp": lax.rem(d + k, n)}, device_id_type=MESH)
    for r in range(1, PIECES):
        pl.semaphore_signal(barrier, inc=1, device_id=peer(r), device_id_type=MESH)
    pl.semaphore_wait(barrier, n - 1 + PIECES - 1)

    def gp_copy(target, source):
        return pltpu.make_async_remote_copy(
            src_ref=gq.at[target], dst_ref=gp.at[source, :, q],
            send_sem=gp_send.at[target], recv_sem=gp_recv.at[source],
            device_id={"dp": target}, device_id_type=MESH,
        )

    def share_copy(image, r, piece):
        return pltpu.make_async_remote_copy(
            src_ref=gp.at[image, :, piece], dst_ref=gp.at[image, :, piece],
            send_sem=sh_send.at[image, r - 1], recv_sem=sh_recv.at[image, r - 1],
            device_id=peer(r), device_id_type=MESH,
        )

    for load in loads[:LIVE]:
        load.wait()

    @pl.loop(1, n)
    def _(k):
        target = lax.rem(d + k, n)
        at = pl.ds(pl.multiple_of(target * cols, cols), cols)
        gate = gate_ref[:, at].astype(F32)
        for t in range(LIVE):
            value = uq[t, :, at].astype(F32) * gate * live(my_base + t)
            gq[target, t] = value.astype(BF16)
        gp_copy(target, d).start()

    for load in loads[LIVE:2 * LIVE]:
        load.wait()
    own_gate = gate_ref[:, own_cols].astype(F32)
    for t in range(LIVE):
        value = uc[t].astype(F32) * own_gate.reshape(1, 1, cols) * live(my_base + t)
        gp[d, t] = value.astype(BF16)
    for load in loads[2 * LIVE:]:
        load.wait()

    def rows_of(image):
        return gp[image].reshape(LIVE * BLOCK, cols)

    def project(image):
        @pl.loop(0, heads // tile)
        def _(j):
            at = pl.ds(pl.multiple_of(j * tile, tile), tile)
            out = lax.dot_general(rows_of(image), w[at, :], (((1,), (1,)), ((), ())), preferred_element_type=F32)
            part[image, pl.ds(base(image), LIVE), :, at] = out.reshape(LIVE, BLOCK, tile)
        part[image, (1 - base(image)) * (BLOCKS - 1)] = jnp.zeros((BLOCK, heads), F32)

    def accumulate(image, read):
        @pl.loop(0, heads // tile)
        def _(j):
            at = pl.ds(pl.multiple_of(j * tile, tile), tile)
            left = read(base(image), at).reshape(LIVE * BLOCK, tile)
            total[at, :] += lax.dot_general(
                left, rows_of(image), (((0,), (0,)), ((), ())), preferred_element_type=F32
            )

    @pl.loop(0, n)
    def _(k):
        @pl.when(k >= 1)
        def _():
            image = lax.rem(d + n - k, n)
            gp_copy(lax.rem(d + k, n), image).wait_recv()
            for r in range(1, PIECES):
                share_copy(image, r, q).start()

        @pl.when(k >= 2)
        def _():
            image = lax.rem(d + n - k + 1, n)
            for r in range(1, PIECES):
                share_copy(image, r, piece_of(r)).wait_recv()
            project(image)

        @pl.when(k == 0)
        def _():
            project(d)

    last = lax.rem(d + 1, n)
    for r in range(1, PIECES):
        share_copy(last, r, piece_of(r)).wait_recv()
    project(last)

    total[...] = jnp.zeros_like(total)
    accumulate(d, lambda first, at: attn[pl.ds(first, LIVE), :, at])

    def chain_copy(step, out, into, send, recv, target):
        return pltpu.make_async_remote_copy(
            src_ref=out.at[step], dst_ref=into.at[step], send_sem=send.at[step], recv_sem=recv.at[step],
            device_id={"dp": target}, device_id_type=MESH,
        )

    steps = half * BLOCKS

    def advance(step, position, shift, into, out, send, recv):
        lane, slot = step // BLOCKS, step % BLOCKS
        target = lax.rem(d + n + shift, n)

        @pl.when(position == 0)
        def _():
            into[step] = jnp.zeros((BLOCK, heads), BF16)

        @pl.when(position > 0)
        def _():
            chain_copy(step, out, into, send, recv, target).wait_recv()

        @pl.when(position < n - 1)
        def _():
            ahead_lo = (shift * (lane - d) > 0).astype(F32)
            ahead_hi = (shift * (lane + half - d) > 0).astype(F32)
            keep = (lax.rem(d, half) == lane).astype(F32) * live(slot)
            value = keep * attn[slot].astype(F32) + (1.0 - keep) * into[step].astype(F32)
            value += ahead_lo * part[lane, slot] + ahead_hi * part[lane + half, slot]
            out[step] = value.astype(BF16)
            chain_copy(step, out, into, send, recv, target).start()

        @pl.when(slot == BLOCKS - 1)
        def _():
            for image in (lane, lane + half):
                @pl.when(shift * (image - d) < 0)
                def _():
                    accumulate(
                        image,
                        lambda first, at: into[pl.ds(lane * BLOCKS + first, LIVE), :, at],
                    )

    @pl.loop(0, steps + n - 1)
    def _(time):
        up, down = time - d, time - (n - 1 - d)

        @pl.when((up >= 0) & (up < steps))
        def _():
            advance(up, d, 1, up_in, up_out, up_send, up_recv)

        @pl.when((down >= 0) & (down < steps))
        def _():
            advance(down, n - 1 - d, -1, dn_in, dn_out, dn_send, dn_recv)

    lane = lax.rem(d, half)
    for t in range(LIVE):
        slot = my_base + t
        at = lane * BLOCKS + slot
        value = up_in[at].astype(F32) + dn_in[at].astype(F32) + part[d, slot]
        ga_ref[block_of(slot)] = (value * live(slot)).astype(BF16)
    ga_ref[BLOCKS - 1] = jnp.zeros((BLOCK, heads), BF16)

    @pl.loop(0, heads // tile)
    def _(j):
        at = pl.ds(pl.multiple_of(j * tile, tile), tile)
        gw_ref[at, :] = (total[at, :] * scale).astype(BF16)

    @pl.loop(1, n)
    def _(k):
        gp_copy(lax.rem(d + k, n), d).wait_send()
        for r in range(1, PIECES):
            share_copy(lax.rem(d + k, n), r, q).wait_send()

    @pl.loop(0, steps)
    def _(step):
        @pl.when(d < n - 1)
        def _():
            chain_copy(step, up_out, up_in, up_send, up_recv, lax.rem(d + 1, n)).wait_send()

        @pl.when(d > 0)
        def _():
            chain_copy(step, dn_out, dn_in, dn_send, dn_recv, lax.rem(d + n - 1, n)).wait_send()


def per_device(upstream, attn, gate, visible, proj_weight):
    slots, width = upstream.shape
    heads, cols = proj_weight.shape
    n = lax.axis_size("dp")
    rows = BLOCK // PIECES
    steps = n // 2 * BLOCKS
    scale = float(1.0 / np.sqrt(np.float32(slots * n)))
    any_space = pl.BlockSpec(memory_space=pl.ANY)
    in_vmem = pl.BlockSpec(memory_space=pltpu.VMEM)
    dma = pltpu.SemaphoreType.DMA
    grad_attn, grad_weight = pl.pallas_call(
        functools.partial(kernel, n, scale),
        out_shape=(
            jax.ShapeDtypeStruct((BLOCKS, BLOCK, heads), BF16),
            jax.ShapeDtypeStruct((heads, cols), BF16),
        ),
        in_specs=[any_space, any_space, in_vmem, pl.BlockSpec(memory_space=pltpu.SMEM), any_space],
        out_specs=(in_vmem, in_vmem),
        scratch_shapes=[
            pltpu.VMEM((LIVE, rows, width), BF16),
            pltpu.VMEM((LIVE, PIECES, rows, cols), BF16),
            pltpu.VMEM((BLOCKS, BLOCK, heads), BF16),
            pltpu.VMEM((heads, cols), BF16),
            pltpu.VMEM((n, LIVE, rows, cols), BF16),
            pltpu.VMEM((n, LIVE, PIECES, rows, cols), BF16),
            pltpu.VMEM((n, BLOCKS, BLOCK, heads), F32),
            pltpu.VMEM((heads, cols), F32),
            pltpu.VMEM((steps, BLOCK, heads), BF16),
            pltpu.VMEM((steps, BLOCK, heads), BF16),
            pltpu.VMEM((steps, BLOCK, heads), BF16),
            pltpu.VMEM((steps, BLOCK, heads), BF16),
            dma((2 * LIVE + 1 + BLOCKS,)),
            dma((n,)), dma((n,)),
            dma((n, PIECES - 1)), dma((n, PIECES - 1)),
            dma((steps,)), dma((steps,)), dma((steps,)), dma((steps,)),
        ],
        compiler_params=pltpu.CompilerParams(
            collective_id=0, has_side_effects=True, vmem_limit_bytes=56 * 1024 * 1024
        ),
    )(
        upstream.reshape(BLOCKS, PIECES, rows, width),
        attn.reshape(BLOCKS, BLOCK, heads),
        gate,
        visible,
        proj_weight,
    )
    return grad_attn.reshape(slots, heads), grad_weight


def solution(mesh):
    return jax.shard_map(
        per_device,
        mesh=mesh,
        in_specs=(
            P(("groups", "dp"), None),
            P(("groups", "dp"), ("mp", "sub")),
            P(("groups", "dp"), None),
            P(("groups", "dp")),
            P(("mp", "sub"), "dp"),
        ),
        out_specs=(P(("groups", "dp"), ("mp", "sub")), P(("mp", "sub"), ("groups", "dp"))),
        check_vma=False,
    )
```

time: 455 us -> 123 us (0.27)
  waiting for transfers between devices: 413 us -> 0 us
  Pallas kernels: 0 us -> 118 us
  matrix products: 21 us -> 0 us
  between operations: 14.7 us -> 1.29 us
    reduce_scatter x1 -> x0, waiting for transfers between devices: 271 us -> none  [per_device(): lax.psum_scatter(lax.dot_general(columns, attn, (((0,), (0,)), ((), ())),...]
    all_gather x1 -> x0, waiting for transfers between devices: 142 us -> none  [per_device(): lax.all_gather(proj_weight, 'dp', axis=1, tiled=True)]
    pallas_call x0 -> x1, Pallas kernels: none -> 118 us  [per_device(): pl.pallas_call(functools.partial(kernel, n, scale), out_shape=(jax.ShapeD...]
    dot_general x2 -> x0, matrix products: 21 us -> none  [the longest x1 10.8 us: per_device(): lax.dot_general(columns, attn, (((0,), (0,)), ((), ())), preferred_elemen...]
  transfers between devices with their start and end apart: 2 -> 0, of which waited for: 2 -> 0; matrix products, arithmetic and copies ran while one was open for 5% -> 0% of each run, Pallas kernels for 0% -> 0%
where the time goes in v1:
time: 123 us
  Pallas kernels  118 us (96%)
  local copies, waits for them, and re-layouts  3.73 us (3%)
  between operations  1.29 us (1%)
    pallas_call x1, Pallas kernels, per_device(): pl.pallas_call(functools.partial(kernel, n, scale), out_shape=(jax.ShapeD...  118 us
    unnamed x4, local copies, waits for them, and re-layouts  3.73 us

profile of v1, /device:TPU:0, one launch (start us, length us, event | category | flops | bytes accessed | tf_op | source)
XLA Modules:
  0.0 123.2 jit_solution(6169631629529744773)
XLA Ops:
  1.3 118.2 %shard_map.68 = (bf16[4,128,1024]{2,1,0:T(8,128)(2,1)}, bf16[1024,1024]{1,0:T(8,128)(2,1)}) custom-call(bf16[4,4,32,4096]{3,2,1,0:T(8,128)(2,1)} %bitcast.3, bf16[4,128,1024]{2,1,0:T(8,128)(2,1)} %bitcast.5, bf16[1,4096]{1,0:T(2,128)(2,1)} %gate_ref.1, s32[1]{0:T(128)S(6)} %copy.9.visible_ref, bf16[1024,1024]{1,0:T(8,128)(2,1)} %w_ref.1), custom_call_target="tpu_custom_call" | custom-call | tf_op jit(solution)/shard_map/pallas_call | solution.py:253
  119.5 0.0 copy-start
  119.5 2.4 %copy.10 = bf16[512,1024]{1,0:T(8,128)(2,1)} copy(bf16[512,1024]{1,0:T(8,128)(2,1)} %bitcast.4) | data formatting | bytes 2097152
  121.9 0.0 copy-done
  121.9 1.3 %copy.11 = bf16[1024,1024]{1,0:T(8,128)(2,1)} copy(bf16[1024,1024]{1,0:T(8,128)(2,1)S(1)} %copy-done) | data formatting | bytes 4194304
Async XLA Ops:
  119.5 2.4 %copy-start = (bf16[1024,1024]{1,0:T(8,128)(2,1)S(1)}, bf16[1024,1024]{1,0:T(8,128)(2,1)}, u32[]{:S(2)}) copy-start(bf16[1024,1024]{1,0:T(8,128)(2,1)} %get-tuple-element.9) | copy-start | bytes 6291460

commit v2 on v1

--- a/solution.py
+++ b/solution.py
@@ -11,6 +11,7 @@
 BLOCK = 128
 BLOCKS = 4
 LIVE = 3
+SPLIT = 1
 PIECES = 4
 MESH = pl.DeviceIdType.MESH
 F32 = jnp.float32
@@ -27,6 +28,7 @@
     half = n // 2
     heads, cols = w_ref.shape
     tile = min(256, heads)
+    thin = BLOCK // SPLIT
     d = lax.axis_index("dp")
     mp = lax.axis_index("mp")
     sub = lax.axis_index("sub")
@@ -85,8 +87,14 @@
         return pltpu.make_async_remote_copy(
             src_ref=gp.at[image, :, piece], dst_ref=gp.at[image, :, piece],
             send_sem=sh_send.at[image, r - 1], recv_sem=sh_recv.at[image, r - 1],
-            device_id=peer(r), device_id_type=MESH,
+            device_id=peer(2 if r == 2 else 1), device_id_type=MESH,
         )
+
+    def finish_share(image):
+        share_copy(image, 2, piece_of(2)).wait_recv()
+        share_copy(image, 3, piece_of(2)).start()
+        share_copy(image, 1, piece_of(1)).wait_recv()
+        share_copy(image, 3, piece_of(3)).wait_recv()
 
     for load in loads[:LIVE]:
         load.wait()
@@ -118,8 +126,8 @@
         def _(j):
             at = pl.ds(pl.multiple_of(j * tile, tile), tile)
             out = lax.dot_general(rows_of(image), w[at, :], (((1,), (1,)), ((), ())), preferred_element_type=F32)
-            part[image, pl.ds(base(image), LIVE), :, at] = out.reshape(LIVE, BLOCK, tile)
-        part[image, (1 - base(image)) * (BLOCKS - 1)] = jnp.zeros((BLOCK, heads), F32)
+            part[image, pl.ds(base(image), LIVE), :, :, at] = out.reshape(LIVE, SPLIT, thin, tile)
+        part[image, (1 - base(image)) * (BLOCKS - 1)] = jnp.zeros((SPLIT, thin, heads), F32)
 
     def accumulate(image, read):
         @pl.loop(0, heads // tile)
@@ -130,20 +138,44 @@
                 left, rows_of(image), (((0,), (0,)), ((), ())), preferred_element_type=F32
             )
 
+    steps = half * BLOCKS * SPLIT
+    pure = (1 - low) * (BLOCKS - 1)
+
+    def chain_copy(step, source, into, send, recv, target):
+        return pltpu.make_async_remote_copy(
+            src_ref=source, dst_ref=into.at[step], send_sem=send.at[step], recv_sem=recv.at[step],
+            device_id={"dp": target}, device_id_type=MESH,
+        )
+
+    def send_pure(position, shift, into, send, recv):
+        @pl.when(position < n - 1)
+        def _():
+            for p in range(SPLIT):
+                step = (lax.rem(d, half) * BLOCKS + pure) * SPLIT + p
+                chain_copy(step, attn.at[pure, p], into, send, recv, lax.rem(d + n + shift, n)).start()
+
     @pl.loop(0, n)
     def _(k):
-        @pl.when(k >= 1)
+        @pl.when(k == n - 1)
         def _():
             image = lax.rem(d + n - k, n)
             gp_copy(lax.rem(d + k, n), image).wait_recv()
-            for r in range(1, PIECES):
-                share_copy(image, r, q).start()
+            share_copy(image, 2, q).start()
+            share_copy(image, 1, q).start()
+            send_pure(d, 1, up_in, up_send, up_recv)
+            send_pure(n - 1 - d, -1, dn_in, dn_send, dn_recv)
+
+        @pl.when((k >= 1) & (k < n - 1))
+        def _():
+            image = lax.rem(d + n - k, n)
+            gp_copy(lax.rem(d + k, n), image).wait_recv()
+            share_copy(image, 2, q).start()
+            share_copy(image, 1, q).start()
 
         @pl.when(k >= 2)
         def _():
             image = lax.rem(d + n - k + 1, n)
-            for r in range(1, PIECES):
-                share_copy(image, r, piece_of(r)).wait_recv()
+            finish_share(image)
             project(image)
 
         @pl.when(k == 0)
@@ -151,56 +183,48 @@
             project(d)
 
     last = lax.rem(d + 1, n)
-    for r in range(1, PIECES):
-        share_copy(last, r, piece_of(r)).wait_recv()
+    finish_share(last)
     project(last)
 
     total[...] = jnp.zeros_like(total)
-    accumulate(d, lambda first, at: attn[pl.ds(first, LIVE), :, at])
-
-    def chain_copy(step, out, into, send, recv, target):
-        return pltpu.make_async_remote_copy(
-            src_ref=out.at[step], dst_ref=into.at[step], send_sem=send.at[step], recv_sem=recv.at[step],
-            device_id={"dp": target}, device_id_type=MESH,
-        )
-
-    steps = half * BLOCKS
+    accumulate(d, lambda first, at: attn[pl.ds(first, LIVE), :, :, at])
 
     def advance(step, position, shift, into, out, send, recv):
-        lane, slot = step // BLOCKS, step % BLOCKS
+        lane, slot, p = step // (BLOCKS * SPLIT), step // SPLIT % BLOCKS, step % SPLIT
         target = lax.rem(d + n + shift, n)
 
         @pl.when(position == 0)
         def _():
-            into[step] = jnp.zeros((BLOCK, heads), BF16)
+            into[step] = jnp.zeros((thin, heads), BF16)
 
         @pl.when(position > 0)
         def _():
-            chain_copy(step, out, into, send, recv, target).wait_recv()
-
-        @pl.when(position < n - 1)
+            chain_copy(step, out.at[step], into, send, recv, target).wait_recv()
+
+        @pl.when((position < n - 1) & ((lane != lax.rem(d, half)) | (slot != pure)))
         def _():
             ahead_lo = (shift * (lane - d) > 0).astype(F32)
             ahead_hi = (shift * (lane + half - d) > 0).astype(F32)
             keep = (lax.rem(d, half) == lane).astype(F32) * live(slot)
-            value = keep * attn[slot].astype(F32) + (1.0 - keep) * into[step].astype(F32)
-            value += ahead_lo * part[lane, slot] + ahead_hi * part[lane + half, slot]
+            value = keep * attn[slot, p].astype(F32) + (1.0 - keep) * into[step].astype(F32)
+            value += ahead_lo * part[lane, slot, p] + ahead_hi * part[lane + half, slot, p]
             out[step] = value.astype(BF16)
-            chain_copy(step, out, into, send, recv, target).start()
-
-        @pl.when(slot == BLOCKS - 1)
+            chain_copy(step, out.at[step], into, send, recv, target).start()
+
+        @pl.when(step % (BLOCKS * SPLIT) == BLOCKS * SPLIT - 1)
         def _():
             for image in (lane, lane + half):
                 @pl.when(shift * (image - d) < 0)
                 def _():
                     accumulate(
                         image,
-                        lambda first, at: into[pl.ds(lane * BLOCKS + first, LIVE), :, at],
+                        lambda first, at: into[pl.ds((lane * BLOCKS + first) * SPLIT, LIVE * SPLIT), :, at],
                     )
 
-    @pl.loop(0, steps + n - 1)
+    @pl.loop(0, max(2 * steps, steps + n - 1))
     def _(time):
-        up, down = time - d, time - (n - 1 - d)
+        up = time - jnp.where(d == n - 1, steps, d)
+        down = time - jnp.where(d == 0, steps, n - 1 - d)
 
         @pl.when((up >= 0) & (up < steps))
         def _():
@@ -213,10 +237,10 @@
     lane = lax.rem(d, half)
     for t in range(LIVE):
         slot = my_base + t
-        at = lane * BLOCKS + slot
+        at = pl.ds((lane * BLOCKS + slot) * SPLIT, SPLIT)
         value = up_in[at].astype(F32) + dn_in[at].astype(F32) + part[d, slot]
         ga_ref[block_of(slot)] = (value * live(slot)).astype(BF16)
-    ga_ref[BLOCKS - 1] = jnp.zeros((BLOCK, heads), BF16)
+    ga_ref[BLOCKS - 1] = jnp.zeros((SPLIT, thin, heads), BF16)
 
     @pl.loop(0, heads // tile)
     def _(j):
@@ -227,17 +251,17 @@
     def _(k):
         gp_copy(lax.rem(d + k, n), d).wait_send()
         for r in range(1, PIECES):
-            share_copy(lax.rem(d + k, n), r, q).wait_send()
+            share_copy(lax.rem(d + k, n), r, piece_of(2) if r == 3 else q).wait_send()
 
     @pl.loop(0, steps)
     def _(step):
         @pl.when(d < n - 1)
         def _():
-            chain_copy(step, up_out, up_in, up_send, up_recv, lax.rem(d + 1, n)).wait_send()
+            chain_copy(step, up_out.at[step], up_in, up_send, up_recv, lax.rem(d + 1, n)).wait_send()
 
         @pl.when(d > 0)
         def _():
-            chain_copy(step, dn_out, dn_in, dn_send, dn_recv, lax.rem(d + n - 1, n)).wait_send()
+            chain_copy(step, dn_out.at[step], dn_in, dn_send, dn_recv, lax.rem(d + n - 1, n)).wait_send()
 
 
 def per_device(upstream, attn, gate, visible, proj_weight):
@@ -245,7 +269,8 @@
     heads, cols = proj_weight.shape
     n = lax.axis_size("dp")
     rows = BLOCK // PIECES
-    steps = n // 2 * BLOCKS
+    steps = n // 2 * BLOCKS * SPLIT
+    thin = BLOCK // SPLIT
     scale = float(1.0 / np.sqrt(np.float32(slots * n)))
     any_space = pl.BlockSpec(memory_space=pl.ANY)
     in_vmem = pl.BlockSpec(memory_space=pltpu.VMEM)
@@ -253,7 +278,7 @@
     grad_attn, grad_weight = pl.pallas_call(
         functools.partial(kernel, n, scale),
         out_shape=(
-            jax.ShapeDtypeStruct((BLOCKS, BLOCK, heads), BF16),
+            jax.ShapeDtypeStruct((BLOCKS, SPLIT, thin, heads), BF16),
             jax.ShapeDtypeStruct((heads, cols), BF16),
         ),
         in_specs=[any_space, any_space, in_vmem, pl.BlockSpec(memory_space=pltpu.SMEM), any_space],
@@ -261,16 +286,16 @@
         scratch_shapes=[
             pltpu.VMEM((LIVE, rows, width), BF16),
             pltpu.VMEM((LIVE, PIECES, rows, cols), BF16),
-            pltpu.VMEM((BLOCKS, BLOCK, heads), BF16),
+            pltpu.VMEM((BLOCKS, SPLIT, thin, heads), BF16),
             pltpu.VMEM((heads, cols), BF16),
             pltpu.VMEM((n, LIVE, rows, cols), BF16),
             pltpu.VMEM((n, LIVE, PIECES, rows, cols), BF16),
-            pltpu.VMEM((n, BLOCKS, BLOCK, heads), F32),
+            pltpu.VMEM((n, BLOCKS, SPLIT, thin, heads), F32),
             pltpu.VMEM((heads, cols), F32),
-            pltpu.VMEM((steps, BLOCK, heads), BF16),
-            pltpu.VMEM((steps, BLOCK, heads), BF16),
-            pltpu.VMEM((steps, BLOCK, heads), BF16),
-            pltpu.VMEM((steps, BLOCK, heads), BF16),
+            pltpu.VMEM((steps, thin, heads), BF16),
+            pltpu.VMEM((steps, thin, heads), BF16),
+            pltpu.VMEM((steps, thin, heads), BF16),
+            pltpu.VMEM((steps, thin, heads), BF16),
             dma((2 * LIVE + 1 + BLOCKS,)),
             dma((n,)), dma((n,)),
             dma((n, PIECES - 1)), dma((n, PIECES - 1)),
@@ -281,7 +306,7 @@
         ),
     )(
         upstream.reshape(BLOCKS, PIECES, rows, width),
-        attn.reshape(BLOCKS, BLOCK, heads),
+        attn.reshape(BLOCKS, SPLIT, thin, heads),
         gate,
         visible,
         proj_weight,

time: 123 us -> 112 us (0.911)
  Pallas kernels: 118 us -> 107 us
    pallas_call x1, Pallas kernels: 118 us -> 107 us  [per_device(): pl.pallas_call(functools.partial(kernel, n, scale), out_shape=(jax.ShapeD...]
where the time goes in v2:
time: 112 us
  Pallas kernels  107 us (96%)
  local copies, waits for them, and re-layouts  3.73 us (3%)
  between operations  1.29 us (1%)
    pallas_call x1, Pallas kernels, per_device(): pl.pallas_call(functools.partial(kernel, n, scale), out_shape=(jax.ShapeD...  107 us
    unnamed x4, local copies, waits for them, and re-layouts  3.73 us

profile of v2, /device:TPU:0, one launch (start us, length us, event | category | flops | bytes accessed | tf_op | source)
XLA Modules:
  0.0 111.6 jit_solution(14299038240888145055)
XLA Ops:
  1.3 106.6 %shard_map.68 = (bf16[4,1,128,1024]{3,2,1,0:T(8,128)(2,1)}, bf16[1024,1024]{1,0:T(8,128)(2,1)}) custom-call(bf16[4,4,32,4096]{3,2,1,0:T(8,128)(2,1)} %bitcast.3, bf16[4,1,128,1024]{3,2,1,0:T(8,128)(2,1)} %bitcast.5, bf16[1,4096]{1,0:T(2,128)(2,1)} %gate_ref.1, s32[1]{0:T(128)S(6)} %copy.9.visible_ref, bf16[1024,1024]{1,0:T(8,128)(2,1)} %w_ref.1), custom_call_target="tpu_custom_call" | custom-call | tf_op jit(solution)/shard_map/pallas_call | solution.py:278
  107.8 0.0 copy-start
  107.8 2.4 %copy.10 = bf16[512,1024]{1,0:T(8,128)(2,1)} copy(bf16[512,1024]{1,0:T(8,128)(2,1)} %bitcast.4) | data formatting | bytes 2097152
  110.3 0.0 copy-done
  110.3 1.3 %copy.11 = bf16[1024,1024]{1,0:T(8,128)(2,1)} copy(bf16[1024,1024]{1,0:T(8,128)(2,1)S(1)} %copy-done) | data formatting | bytes 4194304
Async XLA Ops:
  107.8 2.4 %copy-start = (bf16[1024,1024]{1,0:T(8,128)(2,1)S(1)}, bf16[1024,1024]{1,0:T(8,128)(2,1)}, u32[]{:S(2)}) copy-start(bf16[1024,1024]{1,0:T(8,128)(2,1)} %get-tuple-element.9) | copy-start | bytes 6291460

commit v3 on v2

--- a/solution.py
+++ b/solution.py
@@ -182,12 +182,15 @@
         def _():
             project(d)
 
+        @pl.when(k == 1)
+        def _():
+            total[...] = jnp.zeros_like(total)
+            accumulate(d, lambda first, at: attn[pl.ds(first, LIVE), :, :, at])
+
     last = lax.rem(d + 1, n)
     finish_share(last)
     project(last)
 
-    total[...] = jnp.zeros_like(total)
-    accumulate(d, lambda first, at: attn[pl.ds(first, LIVE), :, :, at])
 
     def advance(step, position, shift, into, out, send, recv):
         lane, slot, p = step // (BLOCKS * SPLIT), step // SPLIT % BLOCKS, step % SPLIT
@@ -211,15 +214,14 @@
             out[step] = value.astype(BF16)
             chain_copy(step, out.at[step], into, send, recv, target).start()
 
-        @pl.when(step % (BLOCKS * SPLIT) == BLOCKS * SPLIT - 1)
-        def _():
-            for image in (lane, lane + half):
-                @pl.when(shift * (image - d) < 0)
-                def _():
-                    accumulate(
-                        image,
-                        lambda first, at: into[pl.ds((lane * BLOCKS + first) * SPLIT, LIVE * SPLIT), :, at],
-                    )
+        image = lane + half * (slot - LIVE + 1)
+
+        @pl.when((slot >= LIVE - 1) & (p == SPLIT - 1) & (shift * (image - d) < 0))
+        def _():
+            accumulate(
+                image,
+                lambda first, at: into[pl.ds((lane * BLOCKS + first) * SPLIT, LIVE * SPLIT), :, at],
+            )
 
     @pl.loop(0, max(2 * steps, steps + n - 1))
     def _(time):

time: 112 us -> 108 us (0.964)
  Pallas kernels: 107 us -> 102 us
    pallas_call x1, Pallas kernels: 107 us -> 102 us  [per_device(): pl.pallas_call(functools.partial(kernel, n, scale), out_shape=(jax.ShapeD...]
where the time goes in v3:
time: 108 us
  Pallas kernels  102 us (94%)
  local copies, waits for them, and re-layouts  3.73 us (3%)
  between operations  1.29 us (1%)
    pallas_call x1, Pallas kernels, per_device(): pl.pallas_call(functools.partial(kernel, n, scale), out_shape=(jax.ShapeD...  102 us
    unnamed x4, local copies, waits for them, and re-layouts  3.73 us

profile of v3, /device:TPU:0, one launch (start us, length us, event | category | flops | bytes accessed | tf_op | source)
XLA Modules:
  0.0 107.5 jit_solution(458784352542726812)
XLA Ops:
  1.3 102.5 %shard_map.68 = (bf16[4,1,128,1024]{3,2,1,0:T(8,128)(2,1)}, bf16[1024,1024]{1,0:T(8,128)(2,1)}) custom-call(bf16[4,4,32,4096]{3,2,1,0:T(8,128)(2,1)} %bitcast.3, bf16[4,1,128,1024]{3,2,1,0:T(8,128)(2,1)} %bitcast.5, bf16[1,4096]{1,0:T(2,128)(2,1)} %gate_ref.1, s32[1]{0:T(128)S(6)} %copy.9.visible_ref, bf16[1024,1024]{1,0:T(8,128)(2,1)} %w_ref.1), custom_call_target="tpu_custom_call" | custom-call | tf_op jit(solution)/shard_map/pallas_call | solution.py:280
  103.8 0.0 copy-start
  103.8 2.4 %copy.10 = bf16[512,1024]{1,0:T(8,128)(2,1)} copy(bf16[512,1024]{1,0:T(8,128)(2,1)} %bitcast.4) | data formatting | bytes 2097152
  106.2 0.0 copy-done
  106.2 1.3 %copy.11 = bf16[1024,1024]{1,0:T(8,128)(2,1)} copy(bf16[1024,1024]{1,0:T(8,128)(2,1)S(1)} %copy-done) | data formatting | bytes 4194304
Async XLA Ops:
  103.8 2.4 %copy-start = (bf16[1024,1024]{1,0:T(8,128)(2,1)S(1)}, bf16[1024,1024]{1,0:T(8,128)(2,1)}, u32[]{:S(2)}) copy-start(bf16[1024,1024]{1,0:T(8,128)(2,1)} %get-tuple-element.9) | copy-start | bytes 6291460
